TPU v7x, 32 devices: a whole 2x2x4 slice. The times are simulated.
32 devices in a mesh: groups: 2 (over x), seq: 16 (over z, y, core).
Axes of the slice: x: 2, y: 2, z: 4, core: 2. Of those that a mesh axis runs over, the one named last changes fastest.
Arguments:
- inputs: bfloat16 [16384, 768], P(('groups', 'seq')), parts along dimension 0, may hold values from -6 to 6
- gates: bfloat16 [16384, 768], P(('groups', 'seq')), parts along dimension 0, may hold values from -6 to 6
- cotangent: bfloat16 [16384, 768], P(('groups', 'seq')), parts along dimension 0, may hold values from -6 to 6
- first_factor: bfloat16 [16, 512, 512], P('seq'), may hold values from -0.25 to 0.25
- second_factor: bfloat16 [512, 16, 16], P('seq'), may hold values from -1.5 to 1.5
- channel_gain: float32 [768], replicated, may hold values from 0.1 to 1.9
Outputs:
- layer_output: bfloat16 [16384, 768], P(('groups', 'seq')), parts along dimension 0
- grad_inputs: bfloat16 [16384, 768], P(('groups', 'seq')), parts along dimension 0
- grad_gates: bfloat16 [16384, 768], P(('groups', 'seq')), parts along dimension 0
- grad_first: bfloat16 [32, 512, 512], P(('groups', 'seq')), parts along dimension 0
- grad_second: bfloat16 [1024, 16, 16], P(('groups', 'seq')), parts along dimension 0
- gain_grad: float32 [1536], P('groups'), parts along dimension 0
There are 2 independent parts, one for each index of `groups`. A program takes and returns all parts, laid end to end along the dimension named above; an argument that names none is the same for every part. Nothing has to cross between parts.
All inputs are finite; a program needn't handle non-finite values.
Results may differ from a plain program's by a relative error of at most 0.0085.
Values may be sent and summed in bfloat16 or wider, within the bound.
A program may use at most 64 MiB of HBM per device.

v0:
```python
import math
import jax
import jax.numpy as jnp
from jax import lax
from jax.sharding import PartitionSpec as P


def lower_mask(extent):
    row_ids = lax.broadcasted_iota(jnp.int32, (extent, extent), 0)
    col_ids = lax.broadcasted_iota(jnp.int32, (extent, extent), 1)
    return col_ids <= row_ids


def on_device(inputs, gates, cotangent, first_factor, second_factor, channel_gain):
    block_count = first_factor.shape[0]
    block_size = first_factor.shape[1]
    channels = inputs.shape[1]
    block_total = second_factor.shape[1]
    rows3 = inputs.reshape(block_count, block_size, channels)
    gates3 = gates.reshape(block_count, block_size, channels)
    upstream3 = cotangent.reshape(block_count, block_size, channels)
    mask_first = lower_mask(block_size)
    mask_second = lower_mask(block_total)
    first_masked = jnp.where(mask_first[None], first_factor, jnp.zeros((), first_factor.dtype))
    second_masked = jnp.where(mask_second[None], second_factor, jnp.zeros((), second_factor.dtype))
    norm_factor = 1.0 / math.sqrt(inputs.shape[0] * lax.axis_size("seq"))
    gates_cols, upstream_cols = (
        lax.all_to_all(gates3, "seq", split_axis=1, concat_axis=0, tiled=True),
        lax.all_to_all(upstream3, "seq", split_axis=1, concat_axis=0, tiled=True),
    )
    first_mixed = jnp.einsum(
        "kab,kbc->kac", first_masked, rows3, preferred_element_type=jnp.float32
    ).astype(jnp.bfloat16)
    columns = lax.all_to_all(first_mixed, "seq", split_axis=1, concat_axis=0, tiled=True)
    second_cols = jnp.einsum(
        "jab,bjc->ajc", second_masked, columns, preferred_element_type=jnp.float32
    ).astype(jnp.bfloat16)
    hidden_values = second_cols.astype(jnp.float32)
    gate_values = gates_cols.astype(jnp.float32)
    upstream_values = upstream_cols.astype(jnp.float32)
    output_cols = (gate_values * channel_gain * hidden_values).astype(jnp.bfloat16)
    hidden_cols = (upstream_values * gate_values * channel_gain).astype(jnp.bfloat16)
    grad_gate_cols = (upstream_values * channel_gain * hidden_values).astype(jnp.bfloat16)
    partial_gain = jnp.sum(upstream_values * gate_values * hidden_values, axis=(0, 1))
    grad_pairs = jnp.einsum(
        "ajc,bjc->jab", hidden_cols, columns, preferred_element_type=jnp.float32
    )
    grad_sec = jnp.where(mask_second[None], grad_pairs, jnp.zeros((), jnp.float32)).astype(
        jnp.bfloat16
    )
    back_cols = jnp.einsum(
        "jab,ajc->bjc", second_masked, hidden_cols, preferred_element_type=jnp.float32
    ).astype(jnp.bfloat16)
    back_rows, output_rows, grad_gate_rows = (
        lax.all_to_all(back_cols, "seq", split_axis=0, concat_axis=1, tiled=True),
        lax.all_to_all(output_cols, "seq", split_axis=0, concat_axis=1, tiled=True),
        lax.all_to_all(grad_gate_cols, "seq", split_axis=0, concat_axis=1, tiled=True),
    )
    gain_grad = lax.psum(partial_gain, "seq") * norm_factor
    grad_pairs_first = jnp.einsum(
        "kac,kbc->kab", back_rows, rows3, preferred_element_type=jnp.float32
    )
    grad_first = jnp.where(mask_first[None], grad_pairs_first, jnp.zeros((), jnp.float32)).astype(
        jnp.bfloat16
    )
    grad_in = jnp.einsum(
        "kab,kac->kbc", first_masked, back_rows, preferred_element_type=jnp.float32
    ).astype(jnp.bfloat16)
    token_rows = inputs.shape[0]
    return (
        output_rows.reshape(token_rows, channels),
        grad_in.reshape(token_rows, channels),
        grad_gate_rows.reshape(token_rows, channels),
        grad_first,
        grad_sec,
        gain_grad,
    )


def solution(mesh):
    placed = (
        P(("groups", "seq"), None),
        P(("groups", "seq"), None),
        P(("groups", "seq"), None),
        P("seq", None, None),
        P("seq", None, None),
        P(),
    )
    return jax.shard_map(
        on_device,
        mesh=mesh,
        in_specs=placed,
        out_specs=(
            P(("groups", "seq"), None),
            P(("groups", "seq"), None),
            P(("groups", "seq"), None),
            P(("groups", "seq"), None, None),
            P(("groups", "seq"), None, None),
            P("groups"),
        ),
        check_vma=False,
    )
```

profile of v0, /device:TPU:0, one launch (start us, length us, event | category | flops | bytes accessed | tf_op | source)
XLA Modules:
  0.0 196.3 jit_solution(10928412952804270693)
XLA Ops:
  0.6 1.1 copy-done
  1.8 1.6 fusion.5
  3.4 1.2 copy.83
  5.1 5.4 %reduce.2 = bf16[512,768]{1,0:T(8,128)(2,1)S(1)} reduce(bf16[512,1,768]{2,1,0:T(2,128)(2,1)S(1)} %bitcast.48, bf16[]{:T(256)} %broadcast.2), dimensions={1}, to_apply=%bitcast.46.reduce_sub_computation | reduce | bytes 1572866
  10.6 1.1 reshape.99
  11.6 7.6 %all-to-all-start.1 = ((bf16[16,2,12288]{2,1,0:T(2,128)(2,1)}), bf16[16,2,12288]{2,1,0:T(2,128)(2,1)}, u32[]{:S(2)}, u32[]{:S(2)}) async-start(bf16[16,2,12288]{2,1,0:T(2,128)(2,1)} %reshape.99), calls=%async_computation.1 | async-start | bytes 1572864 | tf_op jit(solution)/shard_map/all_to_all | solution.py:34
  19.2 1.2 copy.84
  20.4 5.4 %reduce = bf16[512,768]{1,0:T(8,128)(2,1)S(1)} reduce(bf16[512,1,768]{2,1,0:T(2,128)(2,1)S(1)} %bitcast.53, bf16[]{:T(256)} %broadcast.2), dimensions={1}, to_apply=%bitcast.47.reduce_sub_computation | reduce | bytes 1572866
  25.9 1.1 reshape.101
  26.9 11.0 %all-to-all-done.1 = bf16[16,2,12288]{2,1,0:T(2,128)(2,1)} async-done(((bf16[16,2,12288]{2,1,0:T(2,128)(2,1)}), bf16[16,2,12288]{2,1,0:T(2,128)(2,1)}, u32[]{:S(2)}, u32[]{:S(2)}) %all-to-all-start.1) | async-done | bytes 786464 | tf_op jit(solution)/shard_map/all_to_all | solution.py:34
  38.0 5.5 %all-to-all-start = ((bf16[16,2,12288]{2,1,0:T(2,128)(2,1)}), bf16[16,2,12288]{2,1,0:T(2,128)(2,1)}, u32[]{:S(2)}, u32[]{:S(2)}) async-start(bf16[16,2,12288]{2,1,0:T(2,128)(2,1)} %reshape.101), calls=%async_computation | async-start | bytes 1572864 | tf_op jit(solution)/shard_map/all_to_all | solution.py:28
  43.5 1.2 copy.82
  44.7 5.4 %reduce.1 = bf16[512,768]{1,0:T(8,128)(2,1)S(1)} reduce(bf16[512,1,768]{2,1,0:T(2,128)(2,1)S(1)} %bitcast.49, bf16[]{:T(256)} %broadcast.2), dimensions={1}, to_apply=%bitcast.45.reduce_sub_computation | reduce | bytes 1572866
  51.2 11.0 %all-to-all-done = bf16[16,2,12288]{2,1,0:T(2,128)(2,1)} async-done(((bf16[16,2,12288]{2,1,0:T(2,128)(2,1)}), bf16[16,2,12288]{2,1,0:T(2,128)(2,1)}, u32[]{:S(2)}, u32[]{:S(2)}) %all-to-all-start) | async-done | bytes 786464 | tf_op jit(solution)/shard_map/all_to_all | solution.py:28
  62.3 5.5 %all-to-all-start.3 = ((bf16[16,2,12288]{2,1,0:T(2,128)(2,1)}), bf16[16,2,12288]{2,1,0:T(2,128)(2,1)S(1)}, u32[]{:S(2)}, u32[]{:S(2)}) async-start(bf16[16,2,12288]{2,1,0:T(2,128)(2,1)} %reshape.103), calls=%async_computation.3 | async-start | bytes 1572864 | tf_op jit(solution)/shard_map/all_to_all | solution.py:29
  67.9 4.4 %reshape.100 = bf16[512,1,768]{2,1,0:T(2,128)(2,1)S(1)} reshape(bf16[16,2,12288]{2,1,0:T(2,128)(2,1)} %all-to-all-done.1) | data formatting | bytes 1572864
  73.3 4.4 %reshape.102 = bf16[512,1,768]{2,1,0:T(2,128)(2,1)S(1)} reshape(bf16[16,2,12288]{2,1,0:T(2,128)(2,1)} %all-to-all-done) | data formatting | bytes 1572864
  77.8 1.3 convert.3
  79.1 7.3 %all-to-all-done.3 = bf16[16,2,12288]{2,1,0:T(2,128)(2,1)S(1)} async-done(((bf16[16,2,12288]{2,1,0:T(2,128)(2,1)}), bf16[16,2,12288]{2,1,0:T(2,128)(2,1)S(1)}, u32[]{:S(2)}, u32[]{:S(2)}) %all-to-all-start.3) | async-done | bytes 786464 | tf_op jit(solution)/shard_map/all_to_all | solution.py:29
  88.9 2.4 %fusion.2 = (f32[768]{0:T(1024)S(1)}, bf16[16,32,768]{2,0,1:T(8,128)(2,1)S(1)}, bf16[16,32,768]{2,0,1:T(8,128)(2,1)S(1)}, bf16[16,32,768]{2,0,1:T(8,128)(2,1)S(1)}) fusion(f32[16,32,768]{2,1,0:T(8,128)S(1)} %copy-done.1, f32[16,32,768]{2,1,0:T(8,128)S(1)} %convert.4, f32[768]{0:T(1024)S(1)} %copy-done.7, bf16[16,32,768]{2,1,0:T(8,128)(2,1)S(1)} %bitcast.58, ...), kind=kOutput, calls=%fused_computation.5 | convolution fusion | flops 17702144 | bytes 6314240 | tf_op jit(solution)/shard_map/jab,bjc->ajc/dot_general | solution.py:35
  92.7 1.1 copy.54
  93.8 5.5 %all-to-all-start.4 = ((bf16[16,32,768]{2,1,0:T(8,128)(2,1)}), bf16[16,32,768]{2,1,0:T(8,128)(2,1)}, u32[]{:S(2)}, u32[]{:S(2)}) async-start(bf16[16,32,768]{2,1,0:T(8,128)(2,1)} %copy.54), calls=%async_computation.4 | async-start | bytes 1572864 | tf_op jit(solution)/shard_map/all_to_all | solution.py:55
  99.3 1.1 copy.56
  100.5 17.7 %all-to-all-done.4 = bf16[16,32,768]{2,1,0:T(8,128)(2,1)} async-done(((bf16[16,32,768]{2,1,0:T(8,128)(2,1)}), bf16[16,32,768]{2,1,0:T(8,128)(2,1)}, u32[]{:S(2)}, u32[]{:S(2)}) %all-to-all-start.4) | async-done | bytes 786464 | tf_op jit(solution)/shard_map/all_to_all | solution.py:55
  118.1 5.5 %all-to-all-start.5 = ((bf16[16,32,768]{2,1,0:T(8,128)(2,1)}), bf16[16,32,768]{2,1,0:T(8,128)(2,1)S(1)}, u32[]{:S(2)}, u32[]{:S(2)}) async-start(bf16[16,32,768]{2,1,0:T(8,128)(2,1)} %copy.56), calls=%async_computation.5 | async-start | bytes 1572864 | tf_op jit(solution)/shard_map/all_to_all | solution.py:57
  123.6 1.1 copy.48
  124.7 17.6 %all-to-all-done.5 = bf16[16,32,768]{2,1,0:T(8,128)(2,1)S(1)} async-done(((bf16[16,32,768]{2,1,0:T(8,128)(2,1)}), bf16[16,32,768]{2,1,0:T(8,128)(2,1)S(1)}, u32[]{:S(2)}, u32[]{:S(2)}) %all-to-all-start.5) | async-done | bytes 786464 | tf_op jit(solution)/shard_map/all_to_all | solution.py:57
  142.3 5.5 %all-to-all-start.2 = ((bf16[16,32,768]{2,1,0:T(8,128)(2,1)}), bf16[16,32,768]{2,1,0:T(8,128)(2,1)S(1)}, u32[]{:S(2)}, u32[]{:S(2)}) async-start(bf16[16,32,768]{2,1,0:T(8,128)(2,1)} %copy.48), calls=%async_computation.2 | async-start | bytes 1572864 | tf_op jit(solution)/shard_map/all_to_all | solution.py:56
  147.8 1.7 fusion.7
  150.3 38.5 %psum.7 = f32[768]{0:T(1024)S(1)} all-reduce(f32[768]{0:T(1024)S(1)} %get-tuple-element.30), channel_id=1, replica_groups=mesh['groups'=2,'seq'=16] {'seq'}, use_global_device_ids=true, to_apply=%region_1.2 | all-reduce | flops 768 | bytes 6144 | tf_op jit(solution)/shard_map/psum | solution.py:59
  189.4 2.5 %fusion.6 = bf16[1,512,512]{2,1,0:T(8,128)(2,1)} fusion(bf16[512,768]{1,0:T(8,128)(2,1)} %bitcast.10, bf16[512,768]{1,0:T(8,128)(2,1)S(1)} %copy-done), kind=kOutput, calls=%fused_computation.16 | convolution fusion | flops 403439616 | bytes 2097152 | tf_op jit(solution)/shard_map/kac,kbc->kab/dot_general | solution.py:60
  191.9 2.6 %convolution_convert_fusion = bf16[512,768]{1,0:T(8,128)(2,1)} fusion(bf16[512,768]{1,0:T(8,128)(2,1)} %bitcast.10, bf16[1,512,512]{2,1,0:T(8,128)(2,1)S(1)} %copy-done.8), kind=kOutput, calls=%fused_computation.8 | convolution fusion | flops 403570688 | bytes 2097152 | tf_op jit(solution)/shard_map/kab,kac->kbc/dot_general | solution.py:66
  (32 shorter events, 9.8 us)
Async XLA Ops:
  0.6 1.1 copy-start
  11.6 7.6 %copy-start.4 = (bf16[512,768]{1,0:T(8,128)(2,1)S(1)}, bf16[512,768]{1,0:T(8,128)(2,1)}, u32[]{:S(2)}) copy-start(bf16[512,768]{1,0:T(8,128)(2,1)} %param.7) | copy-start | bytes 2359300
  11.6 26.3 %all-to-all-start.1 = ((bf16[16,2,12288]{2,1,0:T(2,128)(2,1)}), bf16[16,2,12288]{2,1,0:T(2,128)(2,1)}, u32[]{:S(2)}, u32[]{:S(2)}) async-start(bf16[16,2,12288]{2,1,0:T(2,128)(2,1)} %reshape.99), calls=%async_computation.1 | async-start | bytes 1572864 | tf_op jit(solution)/shard_map/all_to_all | solution.py:34
  26.9 16.6 %copy-start.5 = (bf16[512,768]{1,0:T(8,128)(2,1)S(1)}, bf16[512,768]{1,0:T(8,128)(2,1)}, u32[]{:S(2)}) copy-start(bf16[512,768]{1,0:T(8,128)(2,1)} %param.8) | copy-start | bytes 2359300
  38.0 24.3 %all-to-all-start = ((bf16[16,2,12288]{2,1,0:T(2,128)(2,1)}), bf16[16,2,12288]{2,1,0:T(2,128)(2,1)}, u32[]{:S(2)}, u32[]{:S(2)}) async-start(bf16[16,2,12288]{2,1,0:T(2,128)(2,1)} %reshape.101), calls=%async_computation | async-start | bytes 1572864 | tf_op jit(solution)/shard_map/all_to_all | solution.py:28
  50.2 17.6 %copy-start.6 = (bf16[32,16,16]{0,2,1:T(8,128)(2,1)S(1)}, bf16[32,16,16]{0,2,1:T(8,128)(2,1)}, u32[]{:S(2)}) copy-start(bf16[32,16,16]{0,2,1:T(8,128)(2,1)} %param.10) | copy-start | bytes 49156
  62.3 24.2 %all-to-all-start.3 = ((bf16[16,2,12288]{2,1,0:T(2,128)(2,1)}), bf16[16,2,12288]{2,1,0:T(2,128)(2,1)S(1)}, u32[]{:S(2)}, u32[]{:S(2)}) async-start(bf16[16,2,12288]{2,1,0:T(2,128)(2,1)} %reshape.103), calls=%async_computation.3 | async-start | bytes 1572864 | tf_op jit(solution)/shard_map/all_to_all | solution.py:29
  87.2 0.7 copy-start.7
  87.3 1.4 copy-start.1
  87.3 1.6 copy-start.2
  91.4 0.9 copy-start.3
  93.8 24.3 %all-to-all-start.4 = ((bf16[16,32,768]{2,1,0:T(8,128)(2,1)}), bf16[16,32,768]{2,1,0:T(8,128)(2,1)}, u32[]{:S(2)}, u32[]{:S(2)}) async-start(bf16[16,32,768]{2,1,0:T(8,128)(2,1)} %copy.54), calls=%async_computation.4 | async-start | bytes 1572864 | tf_op jit(solution)/shard_map/all_to_all | solution.py:55
  118.1 24.2 %all-to-all-start.5 = ((bf16[16,32,768]{2,1,0:T(8,128)(2,1)}), bf16[16,32,768]{2,1,0:T(8,128)(2,1)S(1)}, u32[]{:S(2)}, u32[]{:S(2)}) async-start(bf16[16,32,768]{2,1,0:T(8,128)(2,1)} %copy.56), calls=%async_computation.5 | async-start | bytes 1572864 | tf_op jit(solution)/shard_map/all_to_all | solution.py:57
  142.3 52.2 %all-to-all-start.2 = ((bf16[16,32,768]{2,1,0:T(8,128)(2,1)}), bf16[16,32,768]{2,1,0:T(8,128)(2,1)S(1)}, u32[]{:S(2)}, u32[]{:S(2)}) async-start(bf16[16,32,768]{2,1,0:T(8,128)(2,1)} %copy.48), calls=%async_computation.2 | async-start | bytes 1572864 | tf_op jit(solution)/shard_map/all_to_all | solution.py:56
  149.5 42.4 %copy-start.8 = (bf16[1,512,512]{2,1,0:T(8,128)(2,1)S(1)}, bf16[1,512,512]{2,1,0:T(8,128)(2,1)}, u32[]{:S(2)}) copy-start(bf16[1,512,512]{2,1,0:T(8,128)(2,1)} %param.9) | copy-start | bytes 1572868
where the time goes:
time: 197 us; the launch traced here: 196 us
  waiting for transfers between devices  64.6 us (33%)
  blocking collectives  38.5 us (20%)
  starting transfers between devices  35.1 us (18%)
  local copies, waits for them, and re-layouts  27.5 us (14%)
  other arithmetic  18.3 us (9%)
  matrix products  11.3 us (6%)
    psum x1, blocking collectives, on_device(): gain_grad = lax.psum(partial_gain, 'seq') * norm_factor  38.5 us
    unnamed x30, local copies, waits for them, and re-layouts  20.3 us
    all_to_all x1, waiting for transfers between devices, on_device(): lax.all_to_all(back_cols, 'seq', split_axis=0, concat_axis=1, tiled=True)  17.7 us
    all_to_all x1, waiting for transfers between devices, on_device(): lax.all_to_all(grad_gate_cols, 'seq', split_axis=0, concat_axis=1, tiled=...  17.6 us
    unnamed x3, other arithmetic  16.3 us
    all_to_all x1, waiting for transfers between devices, on_device(): lax.all_to_all(first_mixed, 'seq', split_axis=1, concat_axis=0, tiled=True)  11 us
    all_to_all x1, waiting for transfers between devices, on_device(): lax.all_to_all(gates3, 'seq', split_axis=1, concat_axis=0, tiled=True)  11 us
    all_to_all x1, starting transfers between devices, on_device(): lax.all_to_all(first_mixed, 'seq', split_axis=1, concat_axis=0, tiled=True)  7.57 us
  transfers between devices with their start and end apart: 6, of which 5 were waited for; matrix products, arithmetic and copies ran while one was open for 19% of the time, Pallas kernels for 0%

commit v1 on v0

--- a/solution.py
+++ b/solution.py
@@ -3,6 +3,12 @@
 import jax.numpy as jnp
 from jax import lax
 from jax.sharding import PartitionSpec as P
+
+
+def _unite_scenes(my_tile):
+    next_value = jax.lax.all_gather(my_tile, "seq")
+    f_next = jnp.sum(next_value, axis=0)
+    return f_next
 
 
 def lower_mask(extent):
@@ -56,7 +62,7 @@
         lax.all_to_all(output_cols, "seq", split_axis=0, concat_axis=1, tiled=True),
         lax.all_to_all(grad_gate_cols, "seq", split_axis=0, concat_axis=1, tiled=True),
     )
-    gain_grad = lax.psum(partial_gain, "seq") * norm_factor
+    gain_grad = _unite_scenes(partial_gain) * norm_factor
     grad_pairs_first = jnp.einsum(
         "kac,kbc->kab", back_rows, rows3, preferred_element_type=jnp.float32
     )

time: 197 us -> 186 us (0.944)
  blocking collectives: 38.5 us -> 26.9 us
    psum x1 -> x0, blocking collectives: 38.5 us -> none  [on_device(): gain_grad = lax.psum(partial_gain, 'seq') * norm_factor]
    all_gather x0 -> x1, blocking collectives: none -> 26.9 us  [_unite_scenes(): next_value = jax.lax.all_gather(my_tile, 'seq')]
    unnamed x30 -> x31, local copies, waits for them, and re-layouts: 20.3 us -> 20.3 us
  transfers between devices with their start and end apart: 6 -> 6, of which waited for: 5 -> 5; matrix products, arithmetic and copies ran while one was open for 19% -> 20% of each run, Pallas kernels for 0% -> 0%
where the time goes in v1:
time: 186 us; the launch traced here: 185 us
  waiting for transfers between devices  64.6 us (35%)
  starting transfers between devices  35.1 us (19%)
  local copies, waits for them, and re-layouts  27.5 us (15%)
  blocking collectives  26.9 us (14%)
  other arithmetic  18.4 us (10%)
  matrix products  11.3 us (6%)
    all_gather x1, blocking collectives, _unite_scenes(): next_value = jax.lax.all_gather(my_tile, 'seq')  26.9 us
    unnamed x31, local copies, waits for them, and re-layouts  20.3 us
    all_to_all x1, waiting for transfers between devices, on_device(): lax.all_to_all(back_cols, 'seq', split_axis=0, concat_axis=1, tiled=True)  17.7 us
    all_to_all x1, waiting for transfers between devices, on_device(): lax.all_to_all(grad_gate_cols, 'seq', split_axis=0, concat_axis=1, tiled=...  17.6 us
    unnamed x3, other arithmetic  16.3 us
    all_to_all x1, waiting for transfers between devices, on_device(): lax.all_to_all(first_mixed, 'seq', split_axis=1, concat_axis=0, tiled=True)  11 us
    all_to_all x1, waiting for transfers between devices, on_device(): lax.all_to_all(gates3, 'seq', split_axis=1, concat_axis=0, tiled=True)  11 us
    all_to_all x1, starting transfers between devices, on_device(): lax.all_to_all(first_mixed, 'seq', split_axis=1, concat_axis=0, tiled=True)  7.57 us
  transfers between devices with their start and end apart: 6, of which 5 were waited for; matrix products, arithmetic and copies ran while one was open for 20% of the time, Pallas kernels for 0%

profile of v1, /device:TPU:0, one launch (start us, length us, event | category | flops | bytes accessed | tf_op | source)
XLA Modules:
  0.0 184.7 jit_solution(15634811770722636075)
XLA Ops:
  0.6 1.1 copy-done
  1.8 1.6 fusion.5
  3.4 1.2 copy.83
  5.1 5.4 %reduce.3 = bf16[512,768]{1,0:T(8,128)(2,1)S(1)} reduce(bf16[512,1,768]{2,1,0:T(2,128)(2,1)S(1)} %bitcast.48, bf16[]{:T(256)} %broadcast.2), dimensions={1}, to_apply=%bitcast.46.reduce_sub_computation | reduce | bytes 1572866
  10.6 1.1 reshape.103
  11.6 7.6 %all-to-all-start.1 = ((bf16[16,2,12288]{2,1,0:T(2,128)(2,1)}), bf16[16,2,12288]{2,1,0:T(2,128)(2,1)}, u32[]{:S(2)}, u32[]{:S(2)}) async-start(bf16[16,2,12288]{2,1,0:T(2,128)(2,1)} %reshape.103), calls=%async_computation.1 | async-start | bytes 1572864 | tf_op jit(solution)/shard_map/all_to_all | solution.py:40
  19.2 1.2 copy.84
  20.4 5.4 %reduce.1 = bf16[512,768]{1,0:T(8,128)(2,1)S(1)} reduce(bf16[512,1,768]{2,1,0:T(2,128)(2,1)S(1)} %bitcast.53, bf16[]{:T(256)} %broadcast.2), dimensions={1}, to_apply=%bitcast.47.reduce_sub_computation | reduce | bytes 1572866
  25.9 1.1 reshape.105
  26.9 11.0 %all-to-all-done.1 = bf16[16,2,12288]{2,1,0:T(2,128)(2,1)} async-done(((bf16[16,2,12288]{2,1,0:T(2,128)(2,1)}), bf16[16,2,12288]{2,1,0:T(2,128)(2,1)}, u32[]{:S(2)}, u32[]{:S(2)}) %all-to-all-start.1) | async-done | bytes 786464 | tf_op jit(solution)/shard_map/all_to_all | solution.py:40
  38.0 5.5 %all-to-all-start = ((bf16[16,2,12288]{2,1,0:T(2,128)(2,1)}), bf16[16,2,12288]{2,1,0:T(2,128)(2,1)}, u32[]{:S(2)}, u32[]{:S(2)}) async-start(bf16[16,2,12288]{2,1,0:T(2,128)(2,1)} %reshape.105), calls=%async_computation | async-start | bytes 1572864 | tf_op jit(solution)/shard_map/all_to_all | solution.py:34
  43.5 1.2 copy.82
  44.7 5.4 %reduce.2 = bf16[512,768]{1,0:T(8,128)(2,1)S(1)} reduce(bf16[512,1,768]{2,1,0:T(2,128)(2,1)S(1)} %bitcast.49, bf16[]{:T(256)} %broadcast.2), dimensions={1}, to_apply=%bitcast.45.reduce_sub_computation | reduce | bytes 1572866
  51.2 11.0 %all-to-all-done = bf16[16,2,12288]{2,1,0:T(2,128)(2,1)} async-done(((bf16[16,2,12288]{2,1,0:T(2,128)(2,1)}), bf16[16,2,12288]{2,1,0:T(2,128)(2,1)}, u32[]{:S(2)}, u32[]{:S(2)}) %all-to-all-start) | async-done | bytes 786464 | tf_op jit(solution)/shard_map/all_to_all | solution.py:34
  62.3 5.5 %all-to-all-start.3 = ((bf16[16,2,12288]{2,1,0:T(2,128)(2,1)}), bf16[16,2,12288]{2,1,0:T(2,128)(2,1)S(1)}, u32[]{:S(2)}, u32[]{:S(2)}) async-start(bf16[16,2,12288]{2,1,0:T(2,128)(2,1)} %reshape.107), calls=%async_computation.3 | async-start | bytes 1572864 | tf_op jit(solution)/shard_map/all_to_all | solution.py:35
  67.9 4.4 %reshape.104 = bf16[512,1,768]{2,1,0:T(2,128)(2,1)S(1)} reshape(bf16[16,2,12288]{2,1,0:T(2,128)(2,1)} %all-to-all-done.1) | data formatting | bytes 1572864
  73.3 4.4 %reshape.106 = bf16[512,1,768]{2,1,0:T(2,128)(2,1)S(1)} reshape(bf16[16,2,12288]{2,1,0:T(2,128)(2,1)} %all-to-all-done) | data formatting | bytes 1572864
  77.8 1.3 convert.3
  79.1 7.3 %all-to-all-done.3 = bf16[16,2,12288]{2,1,0:T(2,128)(2,1)S(1)} async-done(((bf16[16,2,12288]{2,1,0:T(2,128)(2,1)}), bf16[16,2,12288]{2,1,0:T(2,128)(2,1)S(1)}, u32[]{:S(2)}, u32[]{:S(2)}) %all-to-all-start.3) | async-done | bytes 786464 | tf_op jit(solution)/shard_map/all_to_all | solution.py:35
  88.9 2.4 %fusion.2 = (f32[768]{0:T(1024)S(1)}, bf16[16,32,768]{2,0,1:T(8,128)(2,1)S(1)}, bf16[16,32,768]{2,0,1:T(8,128)(2,1)S(1)}, bf16[16,32,768]{2,0,1:T(8,128)(2,1)S(1)}) fusion(f32[16,32,768]{2,1,0:T(8,128)S(1)} %copy-done.1, f32[16,32,768]{2,1,0:T(8,128)S(1)} %convert.4, f32[768]{0:T(1024)S(1)} %copy-done.7, bf16[16,32,768]{2,1,0:T(8,128)(2,1)S(1)} %bitcast.58, ...), kind=kOutput, calls=%fused_computation.5 | convolution fusion | flops 17702144 | bytes 6314240 | tf_op jit(solution)/shard_map/jab,bjc->ajc/dot_general | solution.py:41
  92.7 1.1 copy.54
  93.8 5.5 %all-to-all-start.4 = ((bf16[16,32,768]{2,1,0:T(8,128)(2,1)}), bf16[16,32,768]{2,1,0:T(8,128)(2,1)}, u32[]{:S(2)}, u32[]{:S(2)}) async-start(bf16[16,32,768]{2,1,0:T(8,128)(2,1)} %copy.54), calls=%async_computation.4 | async-start | bytes 1572864 | tf_op jit(solution)/shard_map/all_to_all | solution.py:61
  99.3 1.1 copy.56
  100.5 17.7 %all-to-all-done.4 = bf16[16,32,768]{2,1,0:T(8,128)(2,1)} async-done(((bf16[16,32,768]{2,1,0:T(8,128)(2,1)}), bf16[16,32,768]{2,1,0:T(8,128)(2,1)}, u32[]{:S(2)}, u32[]{:S(2)}) %all-to-all-start.4) | async-done | bytes 786464 | tf_op jit(solution)/shard_map/all_to_all | solution.py:61
  118.1 5.5 %all-to-all-start.5 = ((bf16[16,32,768]{2,1,0:T(8,128)(2,1)}), bf16[16,32,768]{2,1,0:T(8,128)(2,1)S(1)}, u32[]{:S(2)}, u32[]{:S(2)}) async-start(bf16[16,32,768]{2,1,0:T(8,128)(2,1)} %copy.56), calls=%async_computation.5 | async-start | bytes 1572864 | tf_op jit(solution)/shard_map/all_to_all | solution.py:63
  123.6 1.1 copy.48
  124.7 17.6 %all-to-all-done.5 = bf16[16,32,768]{2,1,0:T(8,128)(2,1)S(1)} async-done(((bf16[16,32,768]{2,1,0:T(8,128)(2,1)}), bf16[16,32,768]{2,1,0:T(8,128)(2,1)S(1)}, u32[]{:S(2)}, u32[]{:S(2)}) %all-to-all-start.5) | async-done | bytes 786464 | tf_op jit(solution)/shard_map/all_to_all | solution.py:63
  142.3 5.5 %all-to-all-start.2 = ((bf16[16,32,768]{2,1,0:T(8,128)(2,1)}), bf16[16,32,768]{2,1,0:T(8,128)(2,1)S(1)}, u32[]{:S(2)}, u32[]{:S(2)}) async-start(bf16[16,32,768]{2,1,0:T(8,128)(2,1)} %copy.48), calls=%async_computation.2 | async-start | bytes 1572864 | tf_op jit(solution)/shard_map/all_to_all | solution.py:62
  147.8 1.7 fusion.7
  150.3 26.9 %all-gather.1 = f32[16,1,768]{2,1,0:T(1,128)S(1)} all-gather(f32[1,1,768]{2,1,0:T(1,128)S(1)} %reshape.100), channel_id=2, replica_groups=mesh['groups'=2,'seq'=16] {'seq'}, dimensions={0}, use_global_device_ids=true | all-gather | bytes 52224 | tf_op jit(solution)/shard_map/all_gather | solution.py:9
  177.8 2.5 %fusion.6 = bf16[1,512,512]{2,1,0:T(8,128)(2,1)} fusion(bf16[512,768]{1,0:T(8,128)(2,1)} %bitcast.10, bf16[512,768]{1,0:T(8,128)(2,1)S(1)} %copy-done), kind=kOutput, calls=%fused_computation.16 | convolution fusion | flops 403439616 | bytes 2097152 | tf_op jit(solution)/shard_map/kac,kbc->kab/dot_general | solution.py:66
  180.4 2.6 %convolution_convert_fusion = bf16[512,768]{1,0:T(8,128)(2,1)} fusion(bf16[512,768]{1,0:T(8,128)(2,1)} %bitcast.10, bf16[1,512,512]{2,1,0:T(8,128)(2,1)S(1)} %copy-done.8), kind=kOutput, calls=%fused_computation.8 | convolution fusion | flops 403570688 | bytes 2097152 | tf_op jit(solution)/shard_map/kab,kac->kbc/dot_general | solution.py:72
  (34 shorter events, 9.8 us)
Async XLA Ops:
  0.6 1.1 copy-start
  11.6 7.6 %copy-start.4 = (bf16[512,768]{1,0:T(8,128)(2,1)S(1)}, bf16[512,768]{1,0:T(8,128)(2,1)}, u32[]{:S(2)}) copy-start(bf16[512,768]{1,0:T(8,128)(2,1)} %param.7) | copy-start | bytes 2359300
  11.6 26.3 %all-to-all-start.1 = ((bf16[16,2,12288]{2,1,0:T(2,128)(2,1)}), bf16[16,2,12288]{2,1,0:T(2,128)(2,1)}, u32[]{:S(2)}, u32[]{:S(2)}) async-start(bf16[16,2,12288]{2,1,0:T(2,128)(2,1)} %reshape.103), calls=%async_computation.1 | async-start | bytes 1572864 | tf_op jit(solution)/shard_map/all_to_all | solution.py:40
  26.9 16.6 %copy-start.5 = (bf16[512,768]{1,0:T(8,128)(2,1)S(1)}, bf16[512,768]{1,0:T(8,128)(2,1)}, u32[]{:S(2)}) copy-start(bf16[512,768]{1,0:T(8,128)(2,1)} %param.8) | copy-start | bytes 2359300
  38.0 24.3 %all-to-all-start = ((bf16[16,2,12288]{2,1,0:T(2,128)(2,1)}), bf16[16,2,12288]{2,1,0:T(2,128)(2,1)}, u32[]{:S(2)}, u32[]{:S(2)}) async-start(bf16[16,2,12288]{2,1,0:T(2,128)(2,1)} %reshape.105), calls=%async_computation | async-start | bytes 1572864 | tf_op jit(solution)/shard_map/all_to_all | solution.py:34
  50.2 17.6 %copy-start.6 = (bf16[32,16,16]{0,2,1:T(8,128)(2,1)S(1)}, bf16[32,16,16]{0,2,1:T(8,128)(2,1)}, u32[]{:S(2)}) copy-start(bf16[32,16,16]{0,2,1:T(8,128)(2,1)} %param.10) | copy-start | bytes 49156
  62.3 24.2 %all-to-all-start.3 = ((bf16[16,2,12288]{2,1,0:T(2,128)(2,1)}), bf16[16,2,12288]{2,1,0:T(2,128)(2,1)S(1)}, u32[]{:S(2)}, u32[]{:S(2)}) async-start(bf16[16,2,12288]{2,1,0:T(2,128)(2,1)} %reshape.107), calls=%async_computation.3 | async-start | bytes 1572864 | tf_op jit(solution)/shard_map/all_to_all | solution.py:35
  87.2 0.7 copy-start.7
  87.3 1.4 copy-start.1
  87.3 1.6 copy-start.2
  91.4 0.9 copy-start.3
  93.8 24.3 %all-to-all-start.4 = ((bf16[16,32,768]{2,1,0:T(8,128)(2,1)}), bf16[16,32,768]{2,1,0:T(8,128)(2,1)}, u32[]{:S(2)}, u32[]{:S(2)}) async-start(bf16[16,32,768]{2,1,0:T(8,128)(2,1)} %copy.54), calls=%async_computation.4 | async-start | bytes 1572864 | tf_op jit(solution)/shard_map/all_to_all | solution.py:61
  118.1 24.2 %all-to-all-start.5 = ((bf16[16,32,768]{2,1,0:T(8,128)(2,1)}), bf16[16,32,768]{2,1,0:T(8,128)(2,1)S(1)}, u32[]{:S(2)}, u32[]{:S(2)}) async-start(bf16[16,32,768]{2,1,0:T(8,128)(2,1)} %copy.56), calls=%async_computation.5 | async-start | bytes 1572864 | tf_op jit(solution)/shard_map/all_to_all | solution.py:63
  142.3 40.7 %all-to-all-start.2 = ((bf16[16,32,768]{2,1,0:T(8,128)(2,1)}), bf16[16,32,768]{2,1,0:T(8,128)(2,1)S(1)}, u32[]{:S(2)}, u32[]{:S(2)}) async-start(bf16[16,32,768]{2,1,0:T(8,128)(2,1)} %copy.48), calls=%async_computation.2 | async-start | bytes 1572864 | tf_op jit(solution)/shard_map/all_to_all | solution.py:62
  149.5 30.9 %copy-start.8 = (bf16[1,512,512]{2,1,0:T(8,128)(2,1)S(1)}, bf16[1,512,512]{2,1,0:T(8,128)(2,1)}, u32[]{:S(2)}) copy-start(bf16[1,512,512]{2,1,0:T(8,128)(2,1)} %param.9) | copy-start | bytes 1572868
